TPU v7x, 32 devices: a whole 2x2x4 slice. The times are simulated.
32 devices in a mesh: dm: 4 (over y, core), df: 8 (over z, x).
Axes of the slice: x: 2, y: 2, z: 4, core: 2. Of those that a mesh axis runs over, the one named last changes fastest.
Arguments:
- hidden_in: bfloat16 [16, 14848], P(None, 'dm'), may hold values from -30 to 30
- attn_gain: float32 [14848], P('dm'), may hold values from 0.1 to 1.9
- attn_bias: float32 [14848], P('dm'), may hold values from -3 to 3
- mlp_gain: float32 [14848], P('dm'), may hold values from 0.1 to 1.9
- mlp_bias: float32 [14848], P('dm'), may hold values from -3 to 3
- w_query: bfloat16 [14848, 8192], P('dm', 'df'), may hold values from -0.046875 to 0.046875
- query_exp: int32 [464, 8192], P('dm', 'df'), may hold values from -2 to 1
- w_keyval: bfloat16 [14848, 1024], P('dm', 'df'), may hold values from -0.046875 to 0.046875
- keyval_exp: int32 [464, 1024], P('dm', 'df'), may hold values from -2 to 1
- w_out: bfloat16 [8192, 14848], P('df', 'dm'), may hold values from -0.09375 to 0.09375
- out_exp: int32 [256, 14848], P('df', 'dm'), may hold values from -2 to 1
- w_up: bfloat16 [14848, 29696], P('dm', 'df'), may hold values from -0.046875 to 0.046875
- up_exp: int32 [464, 29696], P('dm', 'df'), may hold values from -2 to 1
- w_down: bfloat16 [29696, 14848], P('df', 'dm'), may hold values from -0.046875 to 0.046875
- down_exp: int32 [928, 14848], P('df', 'dm'), may hold values from -2 to 1
- kv_cache: bfloat16 [16, 65536, 128], P('dm', 'df'), may hold values from -384 to 384
- lengths: int32 [16], P('dm'), may hold values from 2 to 8192, as said below
- positions: int32 [16], P('dm'), may hold values from 0 to 32767
Outputs:
- mixed: bfloat16 [16, 14848], P(None, ('dm', 'df'))
Inputs may be any that keep to these rules, and one draw needn't show every extreme that they name: `lengths`: some row uses all 8192 slots.
All inputs are finite; a program needn't handle non-finite values.
Results may differ from a plain program's by a relative error of at most 0.013.
The roundings to bfloat16 on the way count: a program that leaves them out, or rounds other values in their place, can miss the bound.
Values may be sent and summed in bfloat16 or wider, within the bound.
A program may use at most 256 MiB of HBM per device.

v0:
```python
import math

import jax
import jax.numpy as jnp
from jax import lax
from jax.sharding import PartitionSpec as P

D = 14848
HEADS = 128
KV = 8
HD = 64


epsilon = 1e-05


def merged(part, axis, combine):
    gathered = jax.tree.map(lambda a: lax.all_gather(a, axis), part)

    def take(source):
        return jax.tree.map(lambda a: lax.dynamic_index_in_dim(a, source, 0, False), gathered)

    return lax.fori_loop(
        1, lax.axis_size(axis), lambda source, state: combine(state, take(source)), take(0)
    )


def powers(exponents):
    return jnp.where(
        exponents == -2, 0.25, jnp.where(exponents == -1, 0.5, jnp.where(exponents == 0, 1.0, 2.0))
    ).astype(jnp.bfloat16)


def dequantize(weight, exponents):
    depth, width_out = weight.shape
    slabs = weight.reshape(depth // 32, 32, width_out) * powers(exponents)[:, None, :]
    return slabs.reshape(depth, width_out)


def rotate(values, places):
    half = HD // 2
    freqs = jnp.power(10000.0, -2.0 * jnp.arange(half, dtype=jnp.float32) / HD)
    angles = places.astype(jnp.float32)[:, None] * freqs[None, :]
    cosine = jnp.cos(angles)[:, None, :]
    sine = jnp.sin(angles)[:, None, :]
    first_half = values[..., :half]
    second_half = values[..., half:]
    return jnp.concatenate(
        [first_half * cosine - second_half * sine, second_half * cosine + first_half * sine],
        axis=-1,
    )


def join_parts(earlier, later):
    top_early, den_early, acc_early = earlier
    top_late, den_late, acc_late = later
    highest = jnp.maximum(top_early, top_late)
    fade_early = jnp.exp(top_early - highest)
    fade_late = jnp.exp(top_late - highest)
    return (
        highest,
        den_early * fade_early + den_late * fade_late,
        acc_early * fade_early[..., None] + acc_late * fade_late[..., None],
    )


def on_device(
    hidden_in,
    attn_gain,
    attn_bias,
    mlp_gain,
    mlp_bias,
    w_query,
    query_exp,
    w_keyval,
    keyval_exp,
    w_out,
    out_exp,
    w_up,
    up_exp,
    w_down,
    down_exp,
    kv_cache,
    lengths,
    positions,
):
    row_count, local_width = hidden_in.shape
    wide = hidden_in.astype(jnp.float32)
    total_sum, square_sum = lax.psum((jnp.sum(wide, axis=1), jnp.sum(wide * wide, axis=1)), "dm")
    mean_value = (total_sum / D)[:, None]
    inverse = lax.rsqrt(square_sum[:, None] / D - mean_value * mean_value + epsilon)
    normed = (wide - mean_value) * inverse
    attn_in = (normed * attn_gain + attn_bias).astype(jnp.bfloat16)
    mlp_in = (normed * mlp_gain + mlp_bias).astype(jnp.bfloat16)
    query_w = dequantize(w_query, query_exp)
    keyval_w = dequantize(w_keyval, keyval_exp)
    query_cols = query_w.shape[1]
    part_rows = row_count // lax.axis_size("dm")
    projected = lax.psum_scatter(
        jnp.concatenate(
            [
                jnp.dot(attn_in, query_w, preferred_element_type=jnp.float32),
                jnp.dot(attn_in, keyval_w, preferred_element_type=jnp.float32),
            ],
            axis=1,
        ),
        "dm",
        scatter_dimension=0,
        tiled=True,
    )
    query_all, keyval_all = (
        lax.all_gather(projected[:, :query_cols], "df", axis=1, tiled=True),
        lax.all_gather(projected[:, query_cols:], "df", axis=1, tiled=True),
    )
    queries = rotate(query_all.reshape(part_rows, HEADS, HD), positions).astype(jnp.bfloat16)
    keyval_new = keyval_all.reshape(part_rows, KV, 2, HD)
    new_keys = rotate(keyval_new[:, :, 0], positions).astype(jnp.bfloat16)
    new_values = keyval_new[:, :, 1].astype(jnp.bfloat16)
    head_devices = lax.axis_size("df")
    blocks = head_devices // KV
    column = lax.axis_index("df")
    group = column // blocks
    block = column % blocks
    group_size = HEADS // KV
    heads_each = HEADS // head_devices
    slots = kv_cache.shape[1]
    factor = 1.0 / math.sqrt(HD)
    query_group = lax.dynamic_slice_in_dim(
        queries.reshape(part_rows, group_size, KV, HD), group, 1, 2
    )[:, :, 0]
    key_one = lax.dynamic_slice_in_dim(new_keys, group, 1, 1)[:, 0]
    value_one = lax.dynamic_slice_in_dim(new_values, group, 1, 1)[:, 0]
    cache_keys = kv_cache[:, :, :HD]
    cache_values = kv_cache[:, :, HD:]
    scores = (
        jnp.einsum("rgd,rcd->rgc", query_group, cache_keys, preferred_element_type=jnp.float32)
        * factor
    )
    places = block * slots + jnp.arange(slots, dtype=jnp.int32)
    live = (places[None, :] < lengths[:, None])[:, None, :]
    scores = jnp.where(live, scores, -1e30)
    leading = block == 0
    own_scores = (
        jnp.einsum("rgd,rd->rg", query_group, key_one, preferred_element_type=jnp.float32) * factor
    )
    own_scores = jnp.where(leading, own_scores, -1e30)
    top_score = jnp.maximum(jnp.max(scores, axis=-1), own_scores)
    weights = jnp.where(live, jnp.exp(scores - top_score[..., None]), 0.0)
    own_weights = jnp.where(leading, jnp.exp(own_scores - top_score), 0.0)
    denominator = jnp.sum(weights, axis=-1) + own_weights
    summed = jnp.einsum(
        "rgc,rcd->rgd",
        weights.astype(jnp.bfloat16),
        cache_values,
        preferred_element_type=jnp.float32,
    )
    summed = (
        summed
        + own_weights.astype(jnp.bfloat16).astype(jnp.float32)[..., None]
        * value_one.astype(jnp.float32)[:, None, :]
    )
    selector = jnp.arange(KV, dtype=jnp.int32) == group
    acc_full = jnp.where(selector[None, None, :, None], summed[:, :, None, :], 0.0).reshape(
        part_rows, HEADS, HD
    )
    top_full = jnp.where(selector[None, None, :], top_score[:, :, None], -1e30).reshape(
        part_rows, HEADS
    )
    den_full = jnp.where(selector[None, None, :], denominator[:, :, None], 0.0).reshape(
        part_rows, HEADS
    )
    top_all, den_all, acc_all = merged((top_full, den_full, acc_full), "df", join_parts)
    own_acc = lax.dynamic_slice_in_dim(acc_all, column * heads_each, heads_each, 1)
    own_den = lax.dynamic_slice_in_dim(den_all, column * heads_each, heads_each, 1)
    attended = (
        (own_acc / own_den[..., None]).reshape(part_rows, heads_each * HD).astype(jnp.bfloat16)
    )
    out_w = dequantize(w_out, out_exp)
    attention_part = jnp.dot(
        lax.all_gather(attended, "dm", axis=0, tiled=True),
        out_w,
        preferred_element_type=jnp.float32,
    )
    up_w = dequantize(w_up, up_exp)
    down_w = dequantize(w_down, down_exp)
    up_total = lax.psum(jnp.dot(mlp_in, up_w, preferred_element_type=jnp.float32), "dm")
    activated = jax.nn.gelu(up_total, approximate=False).astype(jnp.bfloat16)
    feed_part = jnp.dot(activated, down_w, preferred_element_type=jnp.float32)
    layer_total = lax.psum_scatter(
        attention_part + feed_part, "df", scatter_dimension=1, tiled=True
    )
    slice_width = local_width // head_devices
    residual = lax.dynamic_slice_in_dim(wide, column * slice_width, slice_width, 1)
    return (residual + layer_total).astype(jnp.bfloat16)


def solution(mesh):
    return jax.shard_map(
        on_device,
        mesh=mesh,
        in_specs=(
            P(None, "dm"),
            P("dm"),
            P("dm"),
            P("dm"),
            P("dm"),
            P("dm", "df"),
            P("dm", "df"),
            P("dm", "df"),
            P("dm", "df"),
            P("df", "dm"),
            P("df", "dm"),
            P("dm", "df"),
            P("dm", "df"),
            P("df", "dm"),
            P("df", "dm"),
            P("dm", "df", None),
            P("dm"),
            P("dm"),
        ),
        out_specs=P(None, ("dm", "df")),
        check_vma=False,
    )
```

profile of v0, /device:TPU:0, one launch (start us, length us, event | category | flops | bytes accessed | tf_op | source)
XLA Modules:
  0.0 351.1 jit_solution(15921759953710632095)
XLA Ops:
  6.5 1.0 convert_reduce_fusion
  7.6 1.1 select_convert_fusion.2
  8.7 0.8 select_convert_fusion.4
  9.6 8.4 %all-reduce.1 = (f32[16]{0:T(128)S(1)}, f32[16]{0:T(128)S(1)}) all-reduce(f32[16]{0:T(128)S(1)} %get-tuple-element.199, f32[16]{0:T(128)S(1)} %get-tuple-element.198), channel_id=1, replica_groups=mesh['dm'=4,'df'=8] {'dm'}, use_global_device_ids=true, to_apply=%region_3.0 | all-reduce | flops 32 | bytes 256 | tf_op jit(solution)/shard_map/psum | solution.py:89
  18.0 6.8 %bitcast_multiply_fusion.5 = bf16[3712,1024]{1,0:T(8,128)(2,1)} fusion(bf16[3712,1024]{1,0:T(8,128)(2,1)} %param.25, bf16[116,1024]{1,0:T(8,128)(2,1)S(1)} %select_convert_fusion.2), kind=kLoop, calls=%fused_computation.17 | loop fusion | flops 3801088 | bytes 15441920 | tf_op jit(solution)/shard_map/mul | solution.py:36
  24.9 4.4 %fusion.106 = f32[16,1024]{1,0:T(8,128)S(1)} fusion(bf16[3712,1024]{1,0:T(8,128)(2,1)} %bitcast_multiply_fusion.5, bf16[16,3712]{1,0:T(8,128)(2,1)S(1)} %copy-done, f32[3712]{0:T(1024)S(1)} %copy-done.6, f32[3712]{0:T(1024)S(1)} %copy-done.7, f32[16]{0:T(128)S(1)} %get-tuple-element.233, f32[16]{0:T(128)S(1)} %get-tuple-element.232), kind=kOutput, calls=%fused_computation.167 | convolution fusion | flops 121991168 | bytes 7816320 | tf_op jit(solution)/shard_map/dot_general | solution.py:102
  29.4 0.3 fusion.105
  29.7 0.4 select_convert_fusion.1
  30.1 0.6 pad_maximum_fusion
  30.7 19.0 %bitcast_multiply_fusion.3 = bf16[3712,3712]{1,0:T(8,128)(2,1)} fusion(bf16[3712,3712]{1,0:T(8,128)(2,1)} %param.31, bf16[116,3712]{1,0:T(8,128)(2,1)S(1)} %select_convert_fusion.1), kind=kLoop, calls=%fused_computation.10 | loop fusion | flops 13778944 | bytes 55976960 | tf_op jit(solution)/shard_map/mul | solution.py:36
  49.8 11.6 %fusion.29 = f32[16,3712]{1,0:T(8,128)} fusion(bf16[3712,3712]{1,0:T(8,128)(2,1)} %bitcast_multiply_fusion.3, bf16[16,3712]{1,0:T(8,128)(2,1)S(1)} %copy-done, f32[3712]{0:T(1024)S(1)} %copy-done.8, f32[3712]{0:T(1024)S(1)} %copy-done.9, f32[16]{0:T(128)S(1)} %get-tuple-element.233, f32[16]{0:T(128)S(1)} %get-tuple-element.232), kind=kOutput, calls=%fused_computation.64 | convolution fusion | flops 441282560 | bytes 27944064 | tf_op jit(solution)/shard_map/dot_general | solution.py:186
  61.5 0.1 iota_compare_fusion
  61.7 0.6 dynamic-slice.1
  63.0 0.1 multiply_cosine_fusion
  63.1 30.8 %all-reduce.5.cloned.1.call-done = (f32[16,1152]{1,0:T(8,128)}, f32[16,3712]{1,0:T(8,128)}) async-done(((f32[16,1152]{1,0:T(8,128)}, f32[16,3712]{1,0:T(8,128)}), (f32[16,1152]{1,0:T(8,128)}, f32[16,3712]{1,0:T(8,128)})) %all-reduce.5.cloned.1.call-update) | async-done | bytes 311312
  93.9 0.8 constant_dynamic-slice_fusion.3
  94.7 0.8 dynamic-slice.4
  95.4 26.1 %all_gather.19 = f32[4,1024]{1,0:T(4,128)S(1)} all-gather(f32[4,128]{1,0:T(4,128)S(1)} %dynamic-slice.4), channel_id=1, replica_groups=mesh['dm'=4,'df'=8] {'df'}, dimensions={1}, use_global_device_ids=true | all-gather | bytes 18432 | tf_op jit(solution)/shard_map/all_gather | solution.py:113
  121.6 30.5 %all_gather.18 = f32[4,8192]{1,0:T(4,128)S(1)} all-gather(f32[4,1024]{1,0:T(4,128)S(1)} %constant_dynamic-slice_fusion.3), channel_id=1, replica_groups=mesh['dm'=4,'df'=8] {'df'}, dimensions={1}, use_global_device_ids=true | all-gather | bytes 147456 | tf_op jit(solution)/shard_map/all_gather | solution.py:112
  152.2 0.2 reshape.209
  152.4 0.1 fusion.27
  152.8 0.1 fusion.65
  152.9 5.7 %fusion.108 = (f32[4,16]{1,0:T(4,128)S(1)}, f32[4,16,8192]{2,1,0:T(8,128)S(1)}) fusion(bf16[4,8192,128]{2,1,0:T(8,128)(2,1)} %param.35, bf16[4,16,1,64]{3,1,0,2:T(8,128)(2,1)S(1)} %fusion.64, pred[4,8192]{1,0:T(4,128)(4,1)S(1)} %iota_compare_fusion), kind=kOutput, calls=%fused_computation.168 | convolution fusion | flops 68681664 | bytes 10526976 | tf_op jit(solution)/shard_map/rgd,rcd->rgc/dot_general | solution.py:136
  158.7 0.7 fusion.8
  159.4 6.2 %fusion.9 = f32[4,16,64]{2,1,0:T(8,128)S(1)} fusion(bf16[4,8192,128]{2,1,0:T(8,128)(2,1)} %param.35, f32[4,16,8192]{2,1,0:T(8,128)S(1)} %get-tuple-element.235, f32[4,16]{1,0:T(4,128)S(1)} %multiply_maximum_fusion, pred[4,8192]{1,0:T(4,128)(4,1)S(1)} %iota_compare_fusion, f32[4,64]{1,0:T(4,128)S(1)} %fusion.71, f32[4,16]{1,0:T(4,128)S(1)} %get-tuple-element.226), kind=kOutput, calls=%fused_computation.24 | convolution fusion | flops 68689920 | bytes 10536448 | tf_op jit(solution)/shard_map/rgc,rcd->rgd/dot_general | solution.py:151
  165.6 0.1 bitcast_select_fusion
  165.7 0.8 copy.43
  166.4 0.2 reduce-scatter.4.cloned.1.call-start
  166.8 7.2 %bitcast_multiply_fusion.4 = bf16[1024,3712]{1,0:T(8,128)(2,1)} fusion(bf16[1024,3712]{1,0:T(8,128)(2,1)} %param.29, bf16[32,3712]{1,0:T(8,128)(2,1)S(1)} %select_convert_fusion.3), kind=kLoop, calls=%fused_computation.16 | loop fusion | flops 3801088 | bytes 15441920 | tf_op jit(solution)/shard_map/mul | solution.py:36
  174.0 0.4 select_convert_fusion
  174.4 19.0 %bitcast_multiply_fusion.2 = bf16[3712,3712]{1,0:T(8,128)(2,1)} fusion(bf16[3712,3712]{1,0:T(8,128)(2,1)} %param.33, bf16[116,3712]{1,0:T(8,128)(2,1)S(1)} %select_convert_fusion), kind=kLoop, calls=%fused_computation.9 | loop fusion | flops 13778944 | bytes 55976960 | tf_op jit(solution)/shard_map/mul | solution.py:36
  193.8 26.0 %all_gather.21 = f32[8,4,128]{2,1,0:T(4,128)S(1)} all-gather(f32[1,4,128]{2,1,0:T(4,128)S(1)} %get-tuple-element.230), channel_id=1, replica_groups=mesh['dm'=4,'df'=8] {'df'}, dimensions={0}, use_global_device_ids=true | all-gather | bytes 18432 | tf_op jit(solution)/shard_map/all_gather | solution.py:18
  219.8 26.0 %all_gather.20 = f32[8,4,128]{2,1,0:T(4,128)S(1)} all-gather(f32[1,4,128]{2,1,0:T(4,128)S(1)} %get-tuple-element.231), channel_id=1, replica_groups=mesh['dm'=4,'df'=8] {'df'}, dimensions={0}, use_global_device_ids=true | all-gather | bytes 18432 | tf_op jit(solution)/shard_map/all_gather | solution.py:18
  245.8 0.9 slice_bitcast_fusion
  246.7 0.1 copy.44
  246.8 9.5 %while.19 = (s32[]{:T(128)}, f32[4,128]{1,0:T(4,128)S(1)}, f32[4,128]{1,0:T(4,128)S(1)}, f32[4,128,64]{2,1,0:T(8,128)S(1)}, f32[8,4,128]{2,1,0:T(4,128)S(1)}, /*...) while((s32[]{:T(128)}, f32[4,128]{1,0:T(4,128)S(1)}, ...), condition=%wide.region_8.9_spmd, body=%wide.region_7.8_spmd.sunk | while | flops 101381 | bytes 938135 | solution.py:23
  246.9 0.9 constant_dynamic-slice_fusion.5
  247.8 0.1 copy.66
  247.9 0.3 fusion.119
  248.2 0.9 constant_dynamic-slice_fusion.5
  249.2 0.1 copy.66
  249.3 0.3 fusion.119
  249.6 0.9 constant_dynamic-slice_fusion.5
  250.5 0.1 copy.66
  250.7 0.3 fusion.119
  251.0 0.9 constant_dynamic-slice_fusion.5
  251.9 0.1 copy.66
  252.0 0.3 fusion.119
  252.3 0.9 constant_dynamic-slice_fusion.5
  253.3 0.1 copy.66
  253.4 0.3 fusion.119
  253.7 0.9 constant_dynamic-slice_fusion.5
  254.6 0.1 copy.66
  254.8 0.3 fusion.119
  255.1 0.9 constant_dynamic-slice_fusion.5
  256.0 0.1 copy.66
  256.1 0.3 fusion.119
  256.6 5.2 %all-gather = bf16[4,4,1024]{2,1,0:T(4,128)(2,1)S(1)} all-gather(bf16[1,4,1024]{2,1,0:T(4,128)(2,1)S(1)} %reshape.212), channel_id=1, replica_groups=mesh['dm'=4,'df'=8] {'dm'}, dimensions={0}, use_global_device_ids=true | all-gather | bytes 40960 | tf_op jit(solution)/shard_map/all_gather | solution.py:180
  261.8 4.3 %fusion.109 = f32[16,3712]{1,0:T(8,128)S(1)} fusion(bf16[16,1024]{1,0:T(8,128)(2,1)S(1)} %reshape.213, bf16[1024,3712]{1,0:T(8,128)(2,1)} %bitcast_multiply_fusion.4), kind=kOutput, calls=%fused_computation.169 | convolution fusion | flops 121634816 | bytes 7872512 | tf_op jit(solution)/shard_map/dot_general | solution.py:179
  266.1 11.1 %convolution_add_fusion = f32[16,3712]{1,0:T(8,128)S(1)} fusion(f32[16,3712]{1,0:T(8,128)S(1)} %fusion.109, bf16[3712,3712]{1,0:T(8,128)(2,1)} %bitcast_multiply_fusion.2, f32[16,3712]{1,0:T(8,128)S(1)} %copy-done.5), kind=kOutput, calls=%fused_computation.18 | convolution fusion | flops 444846080 | bytes 28270592 | tf_op jit(solution)/shard_map/dot_general | solution.py:188
  277.3 1.9 copy.48
  279.2 63.6 %reduce-scatter.4.cloned.1.call-done = f32[464,16]{1,0:T(8,128)} async-done(((f32[3712,16]{1,0:T(8,128)}), f32[464,16]{1,0:T(8,128)}) %reduce-scatter.4.cloned.1.call-update) | async-done | bytes 29712
  342.8 1.0 copy.49
  343.8 0.7 add_convert_fusion.4
  (72 shorter events, 1.7 us)
Async XLA Ops:
  6.5 87.4 %all-reduce.5.cloned.1.call-start = ((), (), s32[]{:S(2)}) async-start(), calls=%async_computation.3 | async-start | bytes 622592
  18.0 6.8 %copy-start.3 = (bf16[3712,128]{1,0:T(8,128)(2,1)S(1)}, bf16[3712,128]{1,0:T(8,128)(2,1)}, u32[]{:S(2)}) copy-start(bf16[3712,128]{1,0:T(8,128)(2,1)} %param.27) | copy-start | bytes 2850820
  18.0 6.9 %copy-start = (bf16[16,3712]{1,0:T(8,128)(2,1)S(1)}, bf16[16,3712]{1,0:T(8,128)(2,1)}, u32[]{:S(2)}) copy-start(bf16[16,3712]{1,0:T(8,128)(2,1)} %param.20) | copy-start | bytes 356356
  18.0 6.9 %copy-start.6 = (f32[3712]{0:T(1024)S(1)}, f32[3712]{0:T(1024)}, u32[]{:S(2)}) copy-start(f32[3712]{0:T(1024)} %param.22) | copy-start | bytes 44548
  18.0 6.9 %copy-start.7 = (f32[3712]{0:T(1024)S(1)}, f32[3712]{0:T(1024)}, u32[]{:S(2)}) copy-start(f32[3712]{0:T(1024)} %param.21) | copy-start | bytes 44548
  24.9 4.8 %copy-start.1 = (s32[116,3712]{1,0:T(8,128)S(1)}, s32[116,3712]{1,0:T(8,128)}, u32[]{:S(2)}) copy-start(s32[116,3712]{1,0:T(8,128)} %param.32) | copy-start | bytes 5167108
  30.7 19.0 %copy-start.8 = (f32[3712]{0:T(1024)S(1)}, f32[3712]{0:T(1024)}, u32[]{:S(2)}) copy-start(f32[3712]{0:T(1024)} %param.24) | copy-start | bytes 44548
  30.7 19.0 %copy-start.9 = (f32[3712]{0:T(1024)S(1)}, f32[3712]{0:T(1024)}, u32[]{:S(2)}) copy-start(f32[3712]{0:T(1024)} %param.23) | copy-start | bytes 44548
  49.7 11.7 %copy-start.11 = (s32[4]{0:T(128)S(1)}, s32[4]{0:T(128)}, u32[]{:S(2)}) copy-start(s32[4]{0:T(128)} %param.37) | copy-start | bytes 52
  49.7 11.8 %copy-start.10 = (s32[4]{0:T(128)S(1)}, s32[4]{0:T(128)}, u32[]{:S(2)}) copy-start(s32[4]{0:T(128)} %param.36) | copy-start | bytes 52
  49.7 12.0 %copy-start.12 = (u32[32]{0:T(128)S(1)}, u32[32]{0:T(128)}, u32[]{:S(2)}) copy-start(u32[32]{0:T(128)} %constant.193) | copy-start | bytes 388
  61.4 184.4 %all-gather.3.cloned.1.call-start = ((), (), s32[]{:S(2)}) async-start(), calls=%async_computation.1 | async-start | bytes 1179648 | tf_op jit(solution)/shard_map/all_gather | solution.py:18
  159.4 7.3 %copy-start.4 = (s32[32,3712]{1,0:T(8,128)S(1)}, s32[32,3712]{1,0:T(8,128)}, u32[]{:S(2)}) copy-start(s32[32,3712]{1,0:T(8,128)} %param.30) | copy-start | bytes 1425412
  166.4 176.4 %reduce-scatter.4.cloned.1.call-start = ((), (), s32[]{:S(2)}) async-start(), calls=%async_computation.2 | async-start | bytes 2138112
  166.8 7.2 %copy-start.2 = (s32[116,3712]{1,0:T(8,128)S(1)}, s32[116,3712]{1,0:T(8,128)}, u32[]{:S(2)}) copy-start(s32[116,3712]{1,0:T(8,128)} %param.34) | copy-start | bytes 5167108
  261.8 4.3 %copy-start.5 = (f32[16,3712]{1,0:T(8,128)S(1)}, f32[16,3712]{1,0:T(8,128)}, u32[]{:S(2)}) copy-start(f32[16,3712]{1,0:T(8,128)} %get-tuple-element.217) | copy-start | bytes 712708
Sparse Core Ops, SparseCore 0:
  61.5 32.3 all-reduce.4
  166.6 39.0 all-gather.2
  279.3 63.4 reduce-scatter.3
where the time goes:
time: 352 us; the launch traced here: 351 us
  blocking collectives  122 us (35%)
  waiting for transfers between devices  94.5 us (27%)
  other arithmetic  60.8 us (17%)
  matrix products  43.8 us (12%)
  local copies, waits for them, and re-layouts  15.2 us (4%)
  between operations  14.2 us (4%)
    unnamed x5, waiting for transfers between devices  94.5 us
    mul x5, other arithmetic, dequantize(): weight.reshape(depth // 32, 32, width_out) * powers(exponents)[:, None, :]  52.1 us
    all_gather x2, blocking collectives, merged(): gathered = jax.tree.map(lambda a: lax.all_gather(a, axis), part)  52 us
    all_gather x1, blocking collectives, on_device(): lax.all_gather(projected[:, :query_cols], 'df', axis=1, tiled=True)  30.5 us
    all_gather x1, blocking collectives, on_device(): lax.all_gather(projected[:, query_cols:], 'df', axis=1, tiled=True)  26.1 us
    dot_general x1, matrix products, on_device(): jnp.dot(mlp_in, up_w, preferred_element_type=jnp.float32)  11.6 us
    dot_general x1, matrix products, on_device(): feed_part = jnp.dot(activated, down_w, preferred_element_type=jnp.float32)  11.1 us
    psum x1, blocking collectives, on_device(): lax.psum((jnp.sum(wide, axis=1), jnp.sum(wide * wide, axis=1)), 'dm')  8.37 us
  transfers between devices with their start and end apart: 3, of which 2 were waited for; matrix products, arithmetic and copies ran while one was open for 8% of the time, Pallas kernels for 0%

commit v1 on v0

--- a/solution.py
+++ b/solution.py
@@ -1,8 +1,11 @@
+import functools
 import math
 
 import jax
 import jax.numpy as jnp
 from jax import lax
+from jax.experimental import pallas as pl
+from jax.experimental.pallas import tpu as pltpu
 from jax.sharding import PartitionSpec as P
 
 D = 14848
@@ -194,9 +197,454 @@
     return (residual + layer_total).astype(jnp.bfloat16)
 
 
+BLOCK = 32
+DEEP = 1024
+TILE = 256
+LANES = 128
+F32 = jnp.float32
+BF16 = jnp.bfloat16
+
+
+def pieces(length, step):
+    return [(at, min(step, length - at)) for at in range(0, length, step)]
+
+
+def powers_wide(exponents):
+    return jnp.where(
+        exponents == -2, 0.25, jnp.where(exponents == -1, 0.5, jnp.where(exponents == 0, 1.0, 2.0))
+    )
+
+
+def scaled_tile(left, w_ref, e_ref, start, depth, at, width):
+    total = None
+    for low, span in pieces(depth, TILE):
+        exps = e_ref[pl.ds((start + low) // BLOCK, span // BLOCK), pl.ds(at, width)]
+        scale = jnp.broadcast_to(
+            powers_wide(exps)[:, None, :], (span // BLOCK, BLOCK, width)
+        ).astype(BF16).reshape(span, width)
+        weight = w_ref[pl.ds(start + low, span), pl.ds(at, width)] * scale
+        part = jnp.dot(left[:, low:low + span], weight, preferred_element_type=F32)
+        total = part if total is None else total + part
+    return total
+
+
+def scaled_into(acc_ref, offset, first, left, w_ref, e_ref, start, depth, columns):
+    def one(at, width):
+        value = scaled_tile(left(), w_ref, e_ref, start, depth, at, width)
+        place = pl.ds(offset + at, width)
+        if first:
+            acc_ref[:, place] = value
+        else:
+            acc_ref[:, place] = acc_ref[:, place] + value
+
+    full = columns // TILE
+
+    def step(index, carry):
+        one(pl.multiple_of(index * TILE, TILE), TILE)
+        return carry
+
+    lax.fori_loop(0, full, step, 0)
+    if columns % TILE:
+        one(full * TILE, columns % TILE)
+
+
+def gelu(x):
+    return 0.5 * x * (1.0 + lax.erf(x * (1.0 / math.sqrt(2.0))))
+
+
+def layer_kernel(
+    n_dm, n_df,
+    lengths_ref, hidden_ref, norm_ref, turn_ref,
+    wq_hbm, eq_hbm, wkv_hbm, ekv_hbm, wo_hbm, eo_hbm, wu_hbm, eu_hbm, wd_hbm, ed_hbm, cache_hbm,
+    out_ref,
+    wq, eq, wkv, ekv, wo, eo, wbig, eu, ed, cache,
+    attn_x, mlp_x, resid, stat, qacc, qsend, qrecv, hsend, hrecv, qs, kvn, sc, ob,
+    osend, orecv, aall, att, upacc, upsend, uprecv, act, tot, fsend, frecv,
+    local_sem, s_stat, r_stat, s_q, r_q, s_h, r_h, s_o, r_o, s_a, r_a, s_u, r_u, s_g, r_g, s_f, r_f,
+):
+    rows, width = hidden_ref.shape
+    q_cols = wq.shape[1]
+    units = wu_hbm.shape[1]
+    slots = cache.shape[1]
+    part_rows = rows // n_dm
+    me_m = lax.axis_index("dm")
+    me_f = lax.axis_index("df")
+
+    def along_m(step):
+        return lax.rem(me_m + step, n_dm)
+
+    def along_f(step):
+        return lax.rem(me_f + step, n_df)
+
+    def to_m(source, target, send, recv, step):
+        return pltpu.make_async_remote_copy(
+            src_ref=source, dst_ref=target, send_sem=send.at[step], recv_sem=recv.at[step],
+            device_id=(along_m(step), me_f), device_id_type=pl.DeviceIdType.MESH,
+        )
+
+    def to_f(source, target, send, recv, step):
+        return pltpu.make_async_remote_copy(
+            src_ref=source, dst_ref=target, send_sem=send.at[step], recv_sem=recv.at[step],
+            device_id=(me_m, along_f(step)), device_id_type=pl.DeviceIdType.MESH,
+        )
+
+    def local(source, target, index):
+        return pltpu.make_async_copy(source, target, local_sem.at[index])
+
+    load_q = [local(wq_hbm, wq, 0), local(eq_hbm, eq, 1), local(wkv_hbm, wkv, 2),
+              local(ekv_hbm, ekv, 3)]
+    load_eu = local(eu_hbm, eu, 4)
+    load_ed = local(ed_hbm, ed, 5)
+    load_o = [local(wo_hbm, wo, 6), local(eo_hbm, eo, 7)]
+    load_c = local(cache_hbm, cache, 8)
+    up_parts = pieces(width, DEEP)
+    down_parts = pieces(units, DEEP)
+    load_up = [local(wu_hbm.at[pl.ds(a, s)], wbig.at[pl.ds(a, s)], 9 + i)
+               for i, (a, s) in enumerate(up_parts)]
+    base = 9 + len(up_parts)
+    load_down = [local(wd_hbm.at[pl.ds(a, s)], wbig.at[pl.ds(a, s)], base + i)
+                 for i, (a, s) in enumerate(down_parts)]
+
+    for copy in load_q:
+        copy.start()
+    load_eu.start()
+    load_up[0].start()
+
+    barrier = pltpu.get_barrier_semaphore()
+    for step in range(1, n_dm):
+        pl.semaphore_signal(barrier, inc=1, device_id=(along_m(step), me_f),
+                            device_id_type=pl.DeviceIdType.MESH)
+    for step in range(1, n_df):
+        pl.semaphore_signal(barrier, inc=1, device_id=(me_m, along_f(step)),
+                            device_id_type=pl.DeviceIdType.MESH)
+
+    wide = hidden_ref[...].astype(F32)
+    sums = jnp.sum(wide, axis=1, keepdims=True)
+    squares = jnp.sum(wide * wide, axis=1, keepdims=True)
+    lane16 = lax.broadcasted_iota(jnp.int32, (rows, LANES), 1)
+    stat[0] = jnp.where(lane16 == 0, sums, jnp.where(lane16 == 1, squares, 0.0))
+
+    pl.semaphore_wait(barrier, n_dm - 1 + n_df - 1)
+
+    stat_copies = [to_m(stat.at[0], stat.at[step], s_stat, r_stat, step) for step in range(1, n_dm)]
+    for copy in stat_copies:
+        copy.start()
+    tot[:, :width] = wide
+    tot[:, width:] = jnp.zeros((rows, tot.shape[1] - width), F32)
+    share = width // n_df
+    span = resid.shape[2]
+
+    def window(index):
+        at = index * share
+        low = at // LANES * LANES
+        value = tot[:, low:low + span + LANES]
+        if at > low:
+            value = pltpu.roll(value, span + LANES - (at - low), 1)
+        return value[:, :span]
+
+    for index in range(n_df):
+        resid[index] = window(index)
+    qsend[...] = jnp.zeros_like(qsend)
+    osend[...] = jnp.zeros_like(osend)
+    upacc[:, units:] = jnp.zeros((rows, upacc.shape[1] - units), F32)
+    for copy in stat_copies:
+        copy.wait()
+    both = stat[0]
+    for step in range(1, n_dm):
+        both = both + stat[step]
+    features = float(width * n_dm)
+    mean = both[:, 0:1] / features
+    inverse = lax.rsqrt(both[:, 1:2] / features - mean * mean + epsilon)
+    normed = (hidden_ref[...].astype(F32) - mean) * inverse
+    attn_x[...] = (normed * norm_ref[0:1, :] + norm_ref[1:2, :]).astype(BF16)
+    mlp_x[...] = (normed * norm_ref[2:3, :] + norm_ref[3:4, :]).astype(BF16)
+
+    load_up[1].start()
+    for copy in load_q:
+        copy.wait()
+    for index, (start, depth) in enumerate(up_parts):
+        def left(start=start, depth=depth):
+            return attn_x[:, start:start + depth]
+        scaled_into(qacc, 0, index == 0, left, wq, eq, start, depth, q_cols)
+        scaled_into(qacc, q_cols, index == 0, left, wkv, ekv, start, depth, wkv.shape[1])
+    for index in range(n_dm):
+        qsend[index, 0:part_rows, :] = qacc[index * part_rows:(index + 1) * part_rows, :]
+    q_copies = [to_m(qsend.at[along_m(step)], qrecv.at[step], s_q, r_q, step)
+                for step in range(1, n_dm)]
+    for copy in q_copies:
+        copy.start()
+
+    def up(index):
+        start, depth = up_parts[index]
+        load_up[index].wait()
+        scaled_into(upacc, 0, index == 0, lambda: mlp_x[:, start:start + depth],
+                    wbig, eu, start, depth, units)
+
+    load_up[2].start()
+    load_up[3].start()
+    load_eu.wait()
+    up(0)
+    load_c.start()
+
+    for copy in q_copies:
+        copy.wait()
+    mine = qsend[me_m]
+    for step in range(1, n_dm):
+        mine = mine + qrecv[step]
+    lane = lax.broadcasted_iota(jnp.int32, (8, LANES), 1)
+    low_half = lane < HD
+    cosine = turn_ref[0]
+    sine = turn_ref[1]
+
+    def rope(value):
+        partner = jnp.where(lane % HD < HD // 2, pltpu.roll(value, LANES - HD // 2, 1),
+                            pltpu.roll(value, HD // 2, 1))
+        return value * cosine + partner * sine
+
+    def rounded(value):
+        return value.astype(BF16).astype(F32)
+
+    new = mine[:, q_cols:q_cols + LANES]
+    kvn[...] = rounded(jnp.where(low_half, rope(new), new))
+    roped = [rope(mine[:, at:at + LANES]) for at in range(0, q_cols, LANES)]
+    half = len(roped) // 2
+    for group in range(n_df):
+        early, late = roped[group // 2], roped[half + group // 2]
+        if group % 2 == 0:
+            hsend[group] = jnp.where(low_half, early, pltpu.roll(late, HD, 1))
+        else:
+            hsend[group] = jnp.where(low_half, pltpu.roll(early, HD, 1), late)
+    h_copies = [to_f(hsend.at[along_f(step)], hrecv.at[step], s_h, r_h, step)
+                for step in range(1, n_df)]
+    for copy in h_copies:
+        copy.start()
+
+    load_down[0].start()
+    load_ed.start()
+    up(1)
+    load_down[1].start()
+    up(2)
+    load_down[2].start()
+    for copy in load_o:
+        copy.start()
+    up(3)
+    load_down[3].start()
+    for index in range(n_dm):
+        upsend[index] = upacc[:, index * DEEP:(index + 1) * DEEP].astype(BF16)
+    u_copies = [to_m(upsend.at[along_m(step)], uprecv.at[step], s_u, r_u, step)
+                for step in range(1, n_dm)]
+    for copy in u_copies:
+        copy.start()
+
+    for copy in h_copies:
+        copy.wait()
+    for step in range(n_df):
+        value = hsend[me_f] if step == 0 else hrecv[step]
+        first = jnp.where(low_half, value, 0.0)
+        second = jnp.where(low_half, pltpu.roll(value, HD, 1), 0.0)
+        for row in range(part_rows):
+            at = row * 2 * n_df + 2 * step
+            qs[at:at + 1, :] = first[row:row + 1, :]
+            qs[at + 1:at + 2, :] = second[row:row + 1, :]
+    load_c.wait()
+    heads = 2 * n_df
+    factor = 1.0 / math.sqrt(HD)
+
+    def attend(row, carry):
+        place = pl.ds(pl.multiple_of(row * heads, heads), heads)
+        query = qs[place, :].astype(BF16)
+        own_kv = kvn[pl.ds(row, 1), :]
+        own = jnp.sum(query.astype(F32) * own_kv, axis=1, keepdims=True) * factor
+        top = own
+        limit = lengths_ref[row]
+        for start, depth in pieces(slots, DEEP):
+            score = lax.dot_general(
+                query, cache[row, pl.ds(start, depth), :], (((1,), (1,)), ((), ())),
+                preferred_element_type=F32,
+            ) * factor
+            live = start + lax.broadcasted_iota(jnp.int32, (heads, depth), 1) < limit
+            score = jnp.where(live, score, -1e30)
+            sc[:, pl.ds(start, depth)] = score
+            top = jnp.maximum(top, jnp.max(score, axis=1, keepdims=True))
+        own_weight = jnp.exp(own - top)
+        total = own_weight
+        summed = rounded(own_weight) * own_kv
+        for start, depth in pieces(slots, DEEP):
+            live = start + lax.broadcasted_iota(jnp.int32, (heads, depth), 1) < limit
+            weight = jnp.where(live, jnp.exp(sc[:, pl.ds(start, depth)] - top), 0.0)
+            total = total + jnp.sum(weight, axis=1, keepdims=True)
+            summed = summed + jnp.dot(
+                weight.astype(BF16), cache[row, pl.ds(start, depth), :],
+                preferred_element_type=F32,
+            )
+        ob[place, :] = summed / total
+        return carry
+
+    lax.fori_loop(0, part_rows, attend, 0)
+    for step in range(n_df):
+        for row in range(part_rows):
+            at = row * heads + 2 * step
+            pair = jnp.where(low_half[0:1], pltpu.roll(ob[at:at + 1, :], HD, 1), ob[at + 1:at + 2, :])
+            osend[step, row:row + 1, :] = pair
+    o_copies = [
+        pltpu.make_async_remote_copy(
+            src_ref=osend.at[step], dst_ref=orecv.at[me_f], send_sem=s_o.at[step],
+            recv_sem=r_o.at[step], device_id=(me_m, along_f(n_df - step)),
+            device_id_type=pl.DeviceIdType.MESH,
+        )
+        for step in range(1, n_df)
+    ]
+    for copy in o_copies:
+        copy.start()
+
+    for copy in u_copies:
+        copy.wait()
+    units_mine = upsend[me_m].astype(F32)
+    for step in range(1, n_dm):
+        units_mine = units_mine + uprecv[step].astype(F32)
+    act[me_m] = gelu(units_mine).astype(BF16)
+    g_copies = [to_m(act.at[me_m], act.at[me_m], s_g, r_g, step) for step in range(1, n_dm)]
+    for copy in g_copies:
+        copy.start()
+
+    orecv[me_f] = osend[0]
+    for copy in o_copies:
+        copy.wait()
+    pack = []
+    for index in range(n_df // 2):
+        even, odd = orecv[2 * index], orecv[2 * index + 1]
+        aall[me_m, :, index * LANES:(index + 1) * LANES] = jnp.where(
+            low_half, even, pltpu.roll(odd, HD, 1))
+        at = (half + index) * LANES
+        aall[me_m, :, at:at + LANES] = jnp.where(low_half, pltpu.roll(even, HD, 1), odd)
+    a_copies = [to_m(aall.at[me_m], aall.at[me_m], s_a, r_a, step) for step in range(1, n_dm)]
+    for copy in a_copies:
+        copy.start()
+
+    for copy in g_copies:
+        copy.wait()
+    load_ed.wait()
+
+    def down(index):
+        start, depth = down_parts[index]
+        load_down[index].wait()
+        scaled_into(tot, 0, index == 0, lambda: act[index, :, :depth], wbig, ed, start, depth, width)
+
+    down(0)
+    for copy in a_copies:
+        copy.wait()
+    for index in range(n_dm):
+        att[index * part_rows:(index + 1) * part_rows, :] = aall[index, 0:part_rows, :]
+    for copy in load_o:
+        copy.wait()
+    down(1)
+    scaled_into(tot, 0, False, lambda: att[...].astype(BF16), wo, eo, 0, q_cols, width)
+    down(2)
+    down(3)
+
+    for index in range(n_df):
+        fsend[index] = window(index).astype(BF16)
+    f_copies = [to_f(fsend.at[along_f(step)], frecv.at[step], s_f, r_f, step)
+                for step in range(1, n_df)]
+    for copy in f_copies:
+        copy.start()
+    result = resid[me_f] + fsend[me_f].astype(F32)
+    for step, copy in enumerate(f_copies):
+        copy.wait()
+        result = result + frecv[step + 1].astype(F32)
+    out_ref[...] = result[:, :share].astype(BF16)
+
+
+def fits(mesh, arrays):
+    rows, width = arrays[0].shape
+    n_dm, n_df = mesh.shape["dm"], mesh.shape["df"]
+    local, queries, units = width // n_dm, arrays[5].shape[1] // n_df, arrays[11].shape[1] // n_df
+    return (
+        n_df == KV and HEADS == 16 * KV and queries == DEEP and local == units
+        and rows // n_dm <= 8 and rows % 16 == 0 and local % LANES == 0
+        and len(pieces(local, DEEP)) == 4 and n_dm == 4
+    )
+
+
+def fused(
+    n_dm, n_df, hidden_in, attn_gain, attn_bias, mlp_gain, mlp_bias, w_query, query_exp,
+    w_keyval, keyval_exp, w_out, out_exp, w_up, up_exp, w_down, down_exp, kv_cache, lengths,
+    positions,
+):
+    rows, width = hidden_in.shape
+    part_rows = rows // n_dm
+    norm = jnp.stack([attn_gain, attn_bias, mlp_gain, mlp_bias])
+    half = HD // 2
+    freqs = jnp.power(10000.0, -2.0 * jnp.arange(half, dtype=F32) / HD)
+    angles = positions.astype(F32)[:, None] * freqs[None, :]
+    cosine, sine = jnp.cos(angles), jnp.sin(angles)
+    turn = jnp.stack([
+        jnp.concatenate([cosine] * 4, axis=1), jnp.concatenate([-sine, sine] * 2, axis=1),
+    ])
+    turn = jnp.pad(turn, ((0, 0), (0, 8 - part_rows), (0, 0)))
+    q_cols, kv_cols, units = w_query.shape[1], w_keyval.shape[1], w_up.shape[1]
+    heads = HEADS // KV
+    slots = kv_cache.shape[1]
+    share = width // n_df
+    span = -(-share // LANES) * LANES
+    wide_total = (n_df - 1) * share // LANES * LANES + span + LANES
+    vmem = pltpu.VMEM
+    sem = pltpu.SemaphoreType.DMA
+    scratch = [
+        vmem(w_query.shape, BF16), vmem(query_exp.shape, jnp.int32),
+        vmem(w_keyval.shape, BF16), vmem(keyval_exp.shape, jnp.int32),
+        vmem(w_out.shape, BF16), vmem(out_exp.shape, jnp.int32),
+        vmem((max(width, units), max(width, units)), BF16),
+        vmem(up_exp.shape, jnp.int32), vmem(down_exp.shape, jnp.int32),
+        vmem(kv_cache.shape, BF16),
+        vmem((rows, width), BF16), vmem((rows, width), BF16), vmem((n_df, rows, span), F32),
+        vmem((n_dm, rows, LANES), F32),
+        vmem((rows, q_cols + kv_cols), F32), vmem((n_dm, 8, q_cols + kv_cols), F32),
+        vmem((n_dm, 8, q_cols + kv_cols), F32),
+        vmem((n_df, 8, LANES), F32), vmem((n_df, 8, LANES), F32),
+        vmem((part_rows * heads, LANES), F32), vmem((8, LANES), F32),
+        vmem((heads, slots), F32), vmem((part_rows * heads, LANES), F32),
+        vmem((n_df, 8, LANES), F32), vmem((n_df, 8, LANES), F32),
+        vmem((n_dm, 8, q_cols), F32), vmem((rows, q_cols), F32),
+        vmem((rows, n_dm * DEEP), F32), vmem((n_dm, rows, DEEP), BF16),
+        vmem((n_dm, rows, DEEP), BF16), vmem((n_dm, rows, DEEP), BF16),
+        vmem((rows, wide_total), F32), vmem((n_df, rows, span), BF16),
+        vmem((n_df, rows, span), BF16),
+        sem((17,)),
+        sem((n_dm,)), sem((n_dm,)), sem((n_dm,)), sem((n_dm,)), sem((n_df,)), sem((n_df,)),
+        sem((n_df,)), sem((n_df,)), sem((n_dm,)), sem((n_dm,)), sem((n_dm,)), sem((n_dm,)),
+        sem((n_dm,)), sem((n_dm,)), sem((n_df,)), sem((n_df,)),
+    ]
+    in_vmem = pl.BlockSpec(memory_space=pltpu.VMEM)
+    in_any = pl.BlockSpec(memory_space=pl.ANY)
+    return pl.pallas_call(
+        functools.partial(layer_kernel, n_dm, n_df),
+        out_shape=jax.ShapeDtypeStruct((rows, share), BF16),
+        in_specs=[pl.BlockSpec(memory_space=pltpu.SMEM)] + [in_vmem] * 3 + [in_any] * 11,
+        out_specs=in_vmem,
+        scratch_shapes=scratch,
+        compiler_params=pltpu.CompilerParams(
+            collective_id=0, has_side_effects=True, vmem_limit_bytes=62 * 2**20
+        ),
+    )(
+        lengths, hidden_in, norm, turn, w_query, query_exp, w_keyval, keyval_exp, w_out, out_exp,
+        w_up, up_exp, w_down, down_exp, kv_cache,
+    )
+
+
 def solution(mesh):
+    def whole(*arrays):
+        body = on_device
+        if fits(mesh, arrays):
+            body = functools.partial(fused, mesh.shape["dm"], mesh.shape["df"])
+        return mapped(mesh, body)(*arrays)
+
+    return whole
+
+
+def mapped(mesh, body):
     return jax.shard_map(
-        on_device,
+        body,
         mesh=mesh,
         in_specs=(
             P(None, "dm"),

time: 352 us -> 62.5 us (0.18)
  blocking collectives: 122 us -> 0 us
  waiting for transfers between devices: 94.5 us -> 0 us
  other arithmetic: 60.8 us -> 2.15 us
  Pallas kernels: 0 us -> 55.5 us
  matrix products: 43.8 us -> 0 us
  between operations: 14.2 us -> 0.02 us
  local copies, waits for them, and re-layouts: 15.2 us -> 4.24 us
    all_gather x5 -> x0, blocking collectives: 114 us -> none  [the longest x2 52 us: merged(): gathered = jax.tree.map(lambda a: lax.all_gather(a, axis), part)]
    unnamed x5 -> x0, waiting for transfers between devices: 94.5 us -> none
    pallas_call x0 -> x1, Pallas kernels: none -> 55.5 us  [fused(): pl.pallas_call(functools.partial(layer_kernel, n_dm, n_df), out_shape=jax...]
    mul x6 -> x0, other arithmetic: 52.1 us -> none  [the longest x5 52.1 us: dequantize(): weight.reshape(depth // 32, 32, width_out) * powers(exponents)[:, None, :]]
    dot_general x8 -> x0, matrix products: 43.8 us -> none  [the longest x1 11.6 us: on_device(): jnp.dot(mlp_in, up_w, preferred_element_type=jnp.float32)]
    psum x1 -> x0, blocking collectives: 8.37 us -> none  [on_device(): lax.psum((jnp.sum(wide, axis=1), jnp.sum(wide * wide, axis=1)), 'dm')]
    dynamic_slice x16 -> x0, local copies, waits for them, and re-layouts: 7.42 us -> none  [the longest x14 7.33 us: take(): lax.dynamic_index_in_dim(a, source, 0, False)]
  transfers between devices with their start and end apart: 3 -> 0, of which waited for: 2 -> 0; matrix products, arithmetic and copies ran while one was open for 8% -> 0% of each run, Pallas kernels for 0% -> 0%
where the time goes in v1:
time: 62.5 us; the launch traced here: 61.9 us
  Pallas kernels  55.5 us (89%)
  local copies, waits for them, and re-layouts  4.24 us (7%)
  other arithmetic  2.15 us (3%)
    pallas_call x1, Pallas kernels, fused(): pl.pallas_call(functools.partial(layer_kernel, n_dm, n_df), out_shape=jax...  55.5 us
    another operation x4, local copies, waits for them, and re-layouts, fused(): norm = jnp.stack([attn_gain, attn_bias, mlp_gain, mlp_bias])  2.92 us
    unnamed x1, local copies, waits for them, and re-layouts  1.32 us

profile of v1, /device:TPU:0, one launch (start us, length us, event | category | flops | bytes accessed | tf_op | source)
XLA Modules:
  0.0 61.9 jit_solution(6730515804146782827)
XLA Ops:
  0.0 0.7 %stack.27 = f32[1,3712]{1,0:T(1,128)S(1)} reshape(f32[3712]{0:T(1024)} %param.22) | data formatting | bytes 29696 | tf_op jit(solution)/shard_map/stack | solution.py:576
  0.7 0.7 %stack.26 = f32[1,3712]{1,0:T(1,128)S(1)} reshape(f32[3712]{0:T(1024)} %param.21) | data formatting | bytes 29696 | tf_op jit(solution)/shard_map/stack | solution.py:576
  1.5 0.7 %stack.25 = f32[1,3712]{1,0:T(1,128)S(1)} reshape(f32[3712]{0:T(1024)} %param.20) | data formatting | bytes 29696 | tf_op jit(solution)/shard_map/stack | solution.py:576
  2.2 0.7 %stack.24 = f32[1,3712]{1,0:T(1,128)S(1)} reshape(f32[3712]{0:T(1024)} %param.19) | data formatting | bytes 29696 | tf_op jit(solution)/shard_map/stack | solution.py:576
  2.9 0.7 %pad_maximum_fusion.norm_ref = f32[4,3712]{1,0:T(4,128)} fusion(f32[1,3712]{1,0:T(1,128)S(1)} %stack.27, f32[1,3712]{1,0:T(1,128)S(1)} %stack.26, f32[1,3712]{1,0:T(1,128)S(1)} %stack.25, f32[1,3712]{1,0:T(1,128)S(1)} %stack.24), kind=kLoop, calls=%fused_computation | loop fusion | flops 44544 | bytes 118784 | tf_op jit(solution)/shard_map/stack | solution.py:576
  3.6 0.7 %convert_element_type.5 = f32[4]{0:T(128)S(1)} convert(s32[4]{0:T(128)} %param.35) | non-fusion elementwise | flops 4 | bytes 32 | tf_op jit(solution)/shard_map/convert_element_type | solution.py:579
  4.3 0.1 multiply_cosine_fusion
  4.4 0.1 maximum_bitcast_fusion
  4.5 0.6 select_maximum_fusion.turn_ref
  5.1 55.5 %shard_map.172 = bf16[16,464]{1,0:T(8,128)(2,1)} custom-call(s32[4]{0:T(128)} %lengths_ref.1, bf16[16,3712]{1,0:T(8,128)(2,1)} %hidden_ref.1, f32[4,3712]{1,0:T(4,128)} %pad_maximum_fusion.norm_ref, f32[2,8,128]{2,1,0:T(8,128)} %select_maximum_fusion.turn_ref, bf16[3712,1024]{1,0:T(8,128)(2,1)} %wq_hbm.1, s32[116,1024]{1,0:T(8,128)} %eq_hbm.1, ...), custom_call_target="tpu_custom_call" | custom-call | tf_op jit(solution)/shard_map/pallas_call | solution.py:620
  60.6 1.3 %copy.20 = bf16[16,464]{1,0:T(8,128)(2,1)} copy(bf16[16,464]{1,0:T(8,128)(2,1)} %shard_map.172) | data formatting | bytes 29696
  (1 shorter events, 0.0 us)

commit v2 on v1

--- a/solution.py
+++ b/solution.py
@@ -199,7 +199,9 @@
 
 BLOCK = 32
 DEEP = 1024
-TILE = 256
+TILE = 1024
+DEPTH = 256
+UNROLL = True
 LANES = 128
 F32 = jnp.float32
 BF16 = jnp.bfloat16
@@ -217,7 +219,7 @@
 
 def scaled_tile(left, w_ref, e_ref, start, depth, at, width):
     total = None
-    for low, span in pieces(depth, TILE):
+    for low, span in pieces(depth, DEPTH):
         exps = e_ref[pl.ds((start + low) // BLOCK, span // BLOCK), pl.ds(at, width)]
         scale = jnp.broadcast_to(
             powers_wide(exps)[:, None, :], (span // BLOCK, BLOCK, width)
@@ -243,7 +245,7 @@
         one(pl.multiple_of(index * TILE, TILE), TILE)
         return carry
 
-    lax.fori_loop(0, full, step, 0)
+    lax.fori_loop(0, full, step, 0, unroll=UNROLL)
     if columns % TILE:
         one(full * TILE, columns % TILE)
 
@@ -254,7 +256,7 @@
 
 def layer_kernel(
     n_dm, n_df,
-    lengths_ref, hidden_ref, norm_ref, turn_ref,
+    lengths_ref, positions_ref, hidden_ref, again_ref, abias_ref, mgain_ref, mbias_ref,
     wq_hbm, eq_hbm, wkv_hbm, ekv_hbm, wo_hbm, eo_hbm, wu_hbm, eu_hbm, wd_hbm, ed_hbm, cache_hbm,
     out_ref,
     wq, eq, wkv, ekv, wo, eo, wbig, eu, ed, cache,
@@ -309,6 +311,7 @@
         copy.start()
     load_eu.start()
     load_up[0].start()
+    load_up[1].start()
 
     barrier = pltpu.get_barrier_semaphore()
     for step in range(1, n_dm):
@@ -334,6 +337,9 @@
     share = width // n_df
     span = resid.shape[2]
 
+    def flat(ref):
+        return ref[...].reshape(1, width)
+
     def window(index):
         at = index * share
         low = at // LANES * LANES
@@ -356,17 +362,13 @@
     mean = both[:, 0:1] / features
     inverse = lax.rsqrt(both[:, 1:2] / features - mean * mean + epsilon)
     normed = (hidden_ref[...].astype(F32) - mean) * inverse
-    attn_x[...] = (normed * norm_ref[0:1, :] + norm_ref[1:2, :]).astype(BF16)
-    mlp_x[...] = (normed * norm_ref[2:3, :] + norm_ref[3:4, :]).astype(BF16)
-
-    load_up[1].start()
+    attn_x[...] = (normed * flat(again_ref) + flat(abias_ref)).astype(BF16)
+    mlp_x[...] = (normed * flat(mgain_ref) + flat(mbias_ref)).astype(BF16)
+
     for copy in load_q:
         copy.wait()
-    for index, (start, depth) in enumerate(up_parts):
-        def left(start=start, depth=depth):
-            return attn_x[:, start:start + depth]
-        scaled_into(qacc, 0, index == 0, left, wq, eq, start, depth, q_cols)
-        scaled_into(qacc, q_cols, index == 0, left, wkv, ekv, start, depth, wkv.shape[1])
+    scaled_into(qacc, 0, True, lambda: attn_x[...], wq, eq, 0, width, q_cols)
+    scaled_into(qacc, q_cols, True, lambda: attn_x[...], wkv, ekv, 0, width, wkv.shape[1])
     for index in range(n_dm):
         qsend[index, 0:part_rows, :] = qacc[index * part_rows:(index + 1) * part_rows, :]
     q_copies = [to_m(qsend.at[along_m(step)], qrecv.at[step], s_q, r_q, step)
@@ -385,6 +387,10 @@
     load_eu.wait()
     up(0)
     load_c.start()
+    load_ed.start()
+    load_down[0].start()
+    up(1)
+    load_down[1].start()
 
     for copy in q_copies:
         copy.wait()
@@ -393,8 +399,16 @@
         mine = mine + qrecv[step]
     lane = lax.broadcasted_iota(jnp.int32, (8, LANES), 1)
     low_half = lane < HD
-    cosine = turn_ref[0]
-    sine = turn_ref[1]
+    row8 = lax.broadcasted_iota(jnp.int32, (8, LANES), 0)
+    place8 = jnp.zeros((8, LANES), jnp.int32)
+    for row in range(part_rows):
+        place8 = jnp.where(row8 == row, positions_ref[row], place8)
+    freqs = jnp.zeros((8, LANES), F32)
+    for index in range(HD // 2):
+        freqs = jnp.where(lane % (HD // 2) == index, 10000.0 ** (-2.0 * index / HD), freqs)
+    angles = place8.astype(F32) * freqs
+    cosine = jnp.cos(angles)
+    sine = jnp.where(lane % HD < HD // 2, -1.0, 1.0) * jnp.sin(angles)
 
     def rope(value):
         partner = jnp.where(lane % HD < HD // 2, pltpu.roll(value, LANES - HD // 2, 1),
@@ -419,10 +433,6 @@
     for copy in h_copies:
         copy.start()
 
-    load_down[0].start()
-    load_ed.start()
-    up(1)
-    load_down[1].start()
     up(2)
     load_down[2].start()
     for copy in load_o:
@@ -480,7 +490,19 @@
         ob[place, :] = summed / total
         return carry
 
-    lax.fori_loop(0, part_rows, attend, 0)
+    lax.fori_loop(0, part_rows // 2, attend, 0, unroll=True)
+
+    for copy in u_copies:
+        copy.wait()
+    units_mine = upsend[me_m].astype(F32)
+    for step in range(1, n_dm):
+        units_mine = units_mine + uprecv[step].astype(F32)
+    act[me_m] = gelu(units_mine).astype(BF16)
+    g_copies = [to_m(act.at[me_m], act.at[me_m], s_g, r_g, step) for step in range(1, n_dm)]
+    for copy in g_copies:
+        copy.start()
+
+    lax.fori_loop(part_rows // 2, part_rows, attend, 0, unroll=True)
     for step in range(n_df):
         for row in range(part_rows):
             at = row * heads + 2 * step
@@ -497,20 +519,20 @@
     for copy in o_copies:
         copy.start()
 
-    for copy in u_copies:
-        copy.wait()
-    units_mine = upsend[me_m].astype(F32)
-    for step in range(1, n_dm):
-        units_mine = units_mine + uprecv[step].astype(F32)
-    act[me_m] = gelu(units_mine).astype(BF16)
-    g_copies = [to_m(act.at[me_m], act.at[me_m], s_g, r_g, step) for step in range(1, n_dm)]
     for copy in g_copies:
-        copy.start()
-
+        copy.wait()
+    load_ed.wait()
+
+    def down(index):
+        start, depth = down_parts[index]
+        load_down[index].wait()
+        scaled_into(tot, 0, index == 0, lambda: act[index, :, :depth], wbig, ed, start, depth, width)
+
+    down(0)
+    down(1)
     orecv[me_f] = osend[0]
     for copy in o_copies:
         copy.wait()
-    pack = []
     for index in range(n_df // 2):
         even, odd = orecv[2 * index], orecv[2 * index + 1]
         aall[me_m, :, index * LANES:(index + 1) * LANES] = jnp.where(
@@ -520,26 +542,14 @@
     a_copies = [to_m(aall.at[me_m], aall.at[me_m], s_a, r_a, step) for step in range(1, n_dm)]
     for copy in a_copies:
         copy.start()
-
-    for copy in g_copies:
-        copy.wait()
-    load_ed.wait()
-
-    def down(index):
-        start, depth = down_parts[index]
-        load_down[index].wait()
-        scaled_into(tot, 0, index == 0, lambda: act[index, :, :depth], wbig, ed, start, depth, width)
-
-    down(0)
+    down(2)
     for copy in a_copies:
         copy.wait()
     for index in range(n_dm):
         att[index * part_rows:(index + 1) * part_rows, :] = aall[index, 0:part_rows, :]
     for copy in load_o:
         copy.wait()
-    down(1)
     scaled_into(tot, 0, False, lambda: att[...].astype(BF16), wo, eo, 0, q_cols, width)
-    down(2)
     down(3)
 
     for index in range(n_df):
@@ -573,15 +583,6 @@
 ):
     rows, width = hidden_in.shape
     part_rows = rows // n_dm
-    norm = jnp.stack([attn_gain, attn_bias, mlp_gain, mlp_bias])
-    half = HD // 2
-    freqs = jnp.power(10000.0, -2.0 * jnp.arange(half, dtype=F32) / HD)
-    angles = positions.astype(F32)[:, None] * freqs[None, :]
-    cosine, sine = jnp.cos(angles), jnp.sin(angles)
-    turn = jnp.stack([
-        jnp.concatenate([cosine] * 4, axis=1), jnp.concatenate([-sine, sine] * 2, axis=1),
-    ])
-    turn = jnp.pad(turn, ((0, 0), (0, 8 - part_rows), (0, 0)))
     q_cols, kv_cols, units = w_query.shape[1], w_keyval.shape[1], w_up.shape[1]
     heads = HEADS // KV
     slots = kv_cache.shape[1]
@@ -620,14 +621,14 @@
     return pl.pallas_call(
         functools.partial(layer_kernel, n_dm, n_df),
         out_shape=jax.ShapeDtypeStruct((rows, share), BF16),
-        in_specs=[pl.BlockSpec(memory_space=pltpu.SMEM)] + [in_vmem] * 3 + [in_any] * 11,
+        in_specs=[pl.BlockSpec(memory_space=pltpu.SMEM)] * 2 + [in_vmem] * 5 + [in_any] * 11,
         out_specs=in_vmem,
         scratch_shapes=scratch,
         compiler_params=pltpu.CompilerParams(
             collective_id=0, has_side_effects=True, vmem_limit_bytes=62 * 2**20
         ),
     )(
-        lengths, hidden_in, norm, turn, w_query, query_exp, w_keyval, keyval_exp, w_out, out_exp,
+        lengths, positions, hidden_in, attn_gain, attn_bias, mlp_gain, mlp_bias, w_query, query_exp, w_keyval, keyval_exp, w_out, out_exp,
         w_up, up_exp, w_down, down_exp, kv_cache,
     )
 

time: 62.5 us -> 39.9 us (0.64)
  Pallas kernels: 55.5 us -> 38.4 us
  local copies, waits for them, and re-layouts: 4.24 us -> 1.32 us
  other arithmetic: 2.15 us -> 0 us
    pallas_call x1, Pallas kernels: 55.5 us -> 38.4 us  [fused(): pl.pallas_call(functools.partial(layer_kernel, n_dm, n_df), out_shape=jax...]
    another operation x4 -> x0, local copies, waits for them, and re-layouts: 2.92 us -> none  [fused(): norm = jnp.stack([attn_gain, attn_bias, mlp_gain, mlp_bias])]
    another operation x3 -> x0, other arithmetic: 1.36 us -> none  [the longest x2 0.69 us: fused(): jnp.stack([jnp.concatenate([cosine] * 4, axis=1), jnp.concatenate([-sine,...]
    convert_element_type x1 -> x0, other arithmetic: 0.66 us -> none  [fused(): angles = positions.astype(F32)[:, None] * freqs[None, :]]
where the time goes in v2:
time: 39.9 us; the launch traced here: 39.7 us
  Pallas kernels  38.4 us (96%)
  local copies, waits for them, and re-layouts  1.32 us (3%)
    pallas_call x1, Pallas kernels, fused(): pl.pallas_call(functools.partial(layer_kernel, n_dm, n_df), out_shape=jax...  38.4 us
    unnamed x1, local copies, waits for them, and re-layouts  1.32 us

profile of v2, /device:TPU:0, one launch (start us, length us, event | category | flops | bytes accessed | tf_op | source)
XLA Modules:
  0.0 39.7 jit_solution(14026399824481215451)
XLA Ops:
  0.0 38.4 %shard_map.172 = bf16[16,464]{1,0:T(8,128)(2,1)} custom-call(s32[4]{0:T(128)} %lengths_ref.1, s32[4]{0:T(128)} %positions_ref.1, bf16[16,3712]{1,0:T(8,128)(2,1)} %hidden_ref.1, f32[3712]{0:T(1024)} %again_ref.1, f32[3712]{0:T(1024)} %abias_ref.1, f32[3712]{0:T(1024)} %mgain_ref.1, f32[3712]{0:T(1024)} %mbias_ref.1, bf16[3712,1024]{1,0:T(8,128)(2,1)} %wq_hbm.1, ...), custom_call_target="tpu_custom_call" | custom-call | tf_op jit(solution)/shard_map/pallas_call | solution.py:621
  38.4 1.3 %copy.20 = bf16[16,464]{1,0:T(8,128)(2,1)} copy(bf16[16,464]{1,0:T(8,128)(2,1)} %shard_map.172) | data formatting | bytes 29696
